TPU v7x, 512 devices: a whole 4x4x16 slice. The times are simulated.
512 devices in a mesh: row: 16 (over x, y), col: 32 (over z, core).
Axes of the slice: x: 4, y: 4, z: 16, core: 2. Of those that a mesh axis runs over, the one named last changes fastest.
Arguments:
- species: float32 [512, 256, 2048], P(None, 'col', 'row'), may hold values from -26 to 26, as said below
- start_basis: float32 [512, 256], replicated, may hold values from -6 to 6
Outputs:
- core_fibers: float32 [256, 256, 2048], P('row', 'col')
- basis: float32 [512, 256], replicated
Inputs may be any that keep to these rules, and one draw needn't show every extreme that they name: `species`: entries of the slab.
All inputs are finite; a program needn't handle non-finite values.
Results may differ from a plain program's by a relative error of at most 0.00019.
Values sent between devices are 32-bit elements; how exact they have to be, the bound alone decides.
No kernel may reach another device: no remote copies, remote signals or barrier semaphores. Data moves between devices by JAX's collectives and lax.ppermute only.
A program may use at most 64 MiB of HBM per device.

v0:
```python
import jax
import jax.numpy as jnp
from jax import lax
from jax.sharding import PartitionSpec as P

ITERS = 2


def orthonormalize(applied):
    inner_gram = jnp.dot(
        applied.T, applied, precision=lax.Precision.HIGHEST, preferred_element_type=jnp.float32
    )
    small_lower = jnp.linalg.cholesky(inner_gram)
    return jax.scipy.linalg.solve_triangular(small_lower, applied.T, lower=True).T


def power_steps(tri_lower, start_basis):
    current = start_basis
    for sweep_number in range(ITERS):
        halfway = jnp.dot(
            tri_lower.T,
            current,
            precision=lax.Precision.HIGHEST,
            preferred_element_type=jnp.float32,
        )
        applied = jnp.dot(
            tri_lower, halfway, precision=lax.Precision.HIGHEST, preferred_element_type=jnp.float32
        )
        current = orthonormalize(applied)
    return current


def shards(species, start_basis):
    width_x, cells_z, cells_y = species.shape
    fibers = species.reshape(width_x, cells_z * cells_y)
    local_gram = jnp.dot(
        fibers, fibers.T, precision=lax.Precision.HIGHEST, preferred_element_type=jnp.float32
    )
    gram_sum = lax.psum(local_gram, ("row", "col"))
    basis = power_steps(jnp.linalg.cholesky(gram_sum), start_basis)
    core_flat = jnp.dot(
        basis.T, fibers, precision=lax.Precision.HIGHEST, preferred_element_type=jnp.float32
    )
    core_block = core_flat.reshape(basis.shape[1], cells_z, cells_y)
    core_fibers = lax.all_to_all(core_block, "row", split_axis=0, concat_axis=2, tiled=True)
    return (core_fibers, basis)


def solution(mesh):
    in_specs = (P(None, "col", "row"), P())
    out_specs = (P("row", "col", None), P())
    return jax.shard_map(shards, mesh=mesh, in_specs=in_specs, out_specs=out_specs, check_vma=False)
```

profile of v0, /device:TPU:1, one launch (start us, length us, event | category | flops | bytes accessed | tf_op | source)
XLA Modules:
  0.0 744.2 jit_solution(14799633142379794219)
XLA Ops:
  7.2 7.1 fusion.2
  14.4 2.1 copy.41
  16.4 2.3 copy.25
  18.8 468.0 %all-reduce.4.cloned.1.call-done = f32[512,512]{0,1:T(8,128)} async-done(((f32[512,512]{0,1:T(8,128)}), f32[512,512]{0,1:T(8,128)}) %all-reduce.4.cloned.1.call-update) | async-done | bytes 1048592 | tf_op jit(solution)/shard_map/psum | solution.py:39
  486.8 1.6 copy.19
  488.7 1.0 copy-done.2
  489.7 11.7 %cholesky.136 = f32[128,128]{1,0:T(8,128)S(1)} custom-call(f32[128,128]{1,0:T(8,128)S(1)} %cholesky.407), custom_call_target="Cholesky" | custom-call | tf_op jit(solution)/shard_map/jit(cholesky)/cholesky | solution.py:40
  501.4 9.8 %custom-call.32 = f32[1,128,128]{1,2,0:T(8,128)S(1)} custom-call(f32[1,128,128]{2,1,0:T(8,128)S(1)} %get-tuple-element.62), custom_call_target="InvertDiagBlocksLowerTriangular" | custom-call | tf_op jit(solution)/shard_map/jit(cholesky)/cholesky | solution.py:40
  511.3 1.2 constant_dynamic-update-slice_fusion.5
  512.6 1.3 convolution_subtract_fusion.2
  513.9 11.7 %cholesky.159 = f32[128,128]{1,0:T(8,128)S(1)} custom-call(f32[128,128]{1,0:T(8,128)S(1)} %cholesky.411), custom_call_target="Cholesky" | custom-call | tf_op jit(solution)/shard_map/jit(cholesky)/cholesky | solution.py:40
  525.6 10.0 %custom-call.33 = f32[1,128,128]{1,2,0:T(8,128)S(1)} custom-call(f32[1,128,128]{2,1,0:T(8,128)S(1)} %get-tuple-element.59), custom_call_target="InvertDiagBlocksLowerTriangular" | custom-call | tf_op jit(solution)/shard_map/jit(cholesky)/cholesky | solution.py:40
  535.8 1.3 convolution_subtract_fusion.3
  537.1 11.7 %cholesky.294 = f32[128,128]{1,0:T(8,128)S(1)} custom-call(f32[128,128]{1,0:T(8,128)S(1)} %cholesky.416), custom_call_target="Cholesky" | custom-call | tf_op jit(solution)/shard_map/jit(cholesky)/cholesky | solution.py:40
  548.9 0.7 compare_reduce_fusion.5
  549.5 9.8 %custom-call.39 = f32[1,128,128]{1,2,0:T(8,128)S(1)} custom-call(f32[1,128,128]{2,1,0:T(8,128)S(1)} %get-tuple-element.56), custom_call_target="InvertDiagBlocksLowerTriangular" | custom-call | tf_op jit(solution)/shard_map/jit(cholesky)/cholesky/custom-call.9 | solution.py:40
  559.6 1.2 convolution_subtract_fusion.6
  560.8 11.7 %cholesky.307 = f32[128,128]{1,0:T(8,128)S(1)} custom-call(f32[128,128]{1,0:T(8,128)S(1)} %convolution_subtract_fusion.6), custom_call_target="Cholesky" | custom-call | tf_op jit(solution)/shard_map/jit(cholesky)/cholesky | solution.py:40
  572.6 0.7 compare_reduce_fusion.4
  576.4 1.6 fusion.15
  578.0 1.0 fusion.14
  579.0 1.0 fusion.66
  580.2 11.7 %cholesky.357 = f32[128,128]{1,0:T(8,128)S(1)} custom-call(f32[128,128]{1,0:T(8,128)S(1)} %cholesky.420), custom_call_target="Cholesky" | custom-call | tf_op jit(solution)/shard_map/jit(cholesky)/cholesky | solution.py:13
  592.0 0.6 compare_reduce_fusion.3
  592.6 9.8 %custom-call.40 = f32[1,128,128]{1,2,0:T(8,128)S(1)} custom-call(f32[1,128,128]{2,1,0:T(8,128)S(1)} %get-tuple-element.52), custom_call_target="InvertDiagBlocksLowerTriangular" | custom-call | tf_op jit(solution)/shard_map/jit(cholesky)/cholesky/custom-call.9 | solution.py:13
  603.0 11.8 %cholesky.367 = f32[128,128]{1,0:T(8,128)S(1)} custom-call(f32[128,128]{1,0:T(8,128)S(1)} %convolution_subtract_fusion.5), custom_call_target="Cholesky" | custom-call | tf_op jit(solution)/shard_map/jit(cholesky)/cholesky | solution.py:13
  614.8 0.6 compare_reduce_fusion.2
  616.9 4.0 while.4
  617.5 1.4 bitcast_dynamic-update-slice_fusion.4
  619.5 1.4 bitcast_dynamic-update-slice_fusion.4
  620.9 19.7 %custom-call.41 = f32[2,128,128]{1,2,0:T(8,128)S(1)} custom-call(f32[2,128,128]{2,1,0:T(8,128)S(1)} %get-tuple-element.19), custom_call_target="InvertDiagBlocksLowerTriangular" | custom-call | tf_op jit(solution)/shard_map/jit(_solve_triangular)/triangular_solve | solution.py:14
  642.0 1.2 fusion.7
  643.3 1.0 fusion.13
  644.3 1.0 fusion.67
  645.5 11.7 %cholesky.384 = f32[128,128]{1,0:T(8,128)S(1)} custom-call(f32[128,128]{1,0:T(8,128)S(1)} %cholesky.423), custom_call_target="Cholesky" | custom-call | tf_op jit(solution)/shard_map/jit(cholesky)/cholesky | solution.py:13
  657.9 9.8 %custom-call.42 = f32[1,128,128]{1,2,0:T(8,128)S(1)} custom-call(f32[1,128,128]{2,1,0:T(8,128)S(1)} %get-tuple-element.48), custom_call_target="InvertDiagBlocksLowerTriangular" | custom-call | tf_op jit(solution)/shard_map/jit(cholesky)/cholesky/custom-call.9 | solution.py:13
  668.2 11.9 %cholesky.394 = f32[128,128]{1,0:T(8,128)S(1)} custom-call(f32[128,128]{1,0:T(8,128)S(1)} %convolution_subtract_fusion.4), custom_call_target="Cholesky" | custom-call | tf_op jit(solution)/shard_map/jit(cholesky)/cholesky | solution.py:13
  680.1 0.6 compare_reduce_fusion
  682.1 4.0 while.5
  682.7 1.4 bitcast_dynamic-update-slice_fusion.5
  684.7 1.4 bitcast_dynamic-update-slice_fusion.5
  686.1 19.7 %custom-call.43 = f32[2,128,128]{1,2,0:T(8,128)S(1)} custom-call(f32[2,128,128]{2,1,0:T(8,128)S(1)} %get-tuple-element.20), custom_call_target="InvertDiagBlocksLowerTriangular" | custom-call | tf_op jit(solution)/shard_map/jit(_solve_triangular)/triangular_solve | solution.py:14
  707.3 3.5 fusion.11
  710.8 1.6 copy.26
  712.4 6.2 all-to-all-start
  718.6 1.0 copy.28
  719.6 16.4 %all-to-all-done = f32[256,8,128]{2,1,0:T(8,128)S(1)} async-done(((f32[256,8,128]{2,1,0:T(8,128)}), f32[256,8,128]{2,1,0:T(8,128)S(1)}, u32[]{:S(2)}, u32[]{:S(2)}) %all-to-all-start) | async-done | bytes 1048608 | tf_op jit(solution)/shard_map/all_to_all | solution.py:45
  736.1 1.1 copy.42
  (57 shorter events, 9.2 us)
Async XLA Ops:
  7.2 569.2 %copy-start = (f32[512,256]{1,0:T(8,128)S(1)}, f32[512,256]{1,0:T(8,128)}, u32[]{:S(2)}) copy-start(f32[512,256]{1,0:T(8,128)} %param.8) | copy-start | bytes 1572868
  7.2 479.6 %all-reduce.4.cloned.1.call-start = ((), (), s32[]{:S(2)}) async-start(), calls=%async_computation.1 | async-start | bytes 2097152 | tf_op jit(solution)/shard_map/psum | solution.py:39
  486.8 1.7 copy-start.1
  488.7 1.0 copy-start.2
  712.4 23.7 %all-to-all-start = ((f32[256,8,128]{2,1,0:T(8,128)}), f32[256,8,128]{2,1,0:T(8,128)S(1)}, u32[]{:S(2)}, u32[]{:S(2)}) async-start(f32[256,8,128]{2,1,0:T(8,128)} %copy.26), calls=%async_computation | async-start | bytes 2097152 | tf_op jit(solution)/shard_map/all_to_all | solution.py:45
Sparse Core Ops, SparseCore 0:
  14.5 472.2 all-reduce.3
where the time goes:
time: 749 us; the launch traced here: 744 us
  waiting for transfers between devices  484 us (65%)
  other arithmetic  188 us (25%)
  matrix products  26.7 us (4%)
  between operations  19.8 us (3%)
  local copies, waits for them, and re-layouts  19.1 us (3%)
    psum x1, waiting for transfers between devices, shards(): gram_sum = lax.psum(local_gram, ('row', 'col'))  468 us
    another operation x14, other arithmetic, shards(): basis = power_steps(jnp.linalg.cholesky(gram_sum), start_basis)  78.5 us
    another operation x14, other arithmetic, orthonormalize(): small_lower = jnp.linalg.cholesky(inner_gram)  69.5 us
    another operation x5, other arithmetic, orthonormalize(): jax.scipy.linalg.solve_triangular(small_lower, applied.T, lower=True)  39.4 us
    all_to_all x1, waiting for transfers between devices, shards(): lax.all_to_all(core_block, 'row', split_axis=0, concat_axis=2, tiled=True)  16.4 us
  transfers between devices with their start and end apart: 2, of which 2 were waited for; matrix products, arithmetic and copies ran while one was open for 1% of the time, Pallas kernels for 0%

commit v1 on v0

--- a/solution.py
+++ b/solution.py
@@ -42,7 +42,15 @@
         basis.T, fibers, precision=lax.Precision.HIGHEST, preferred_element_type=jnp.float32
     )
     core_block = core_flat.reshape(basis.shape[1], cells_z, cells_y)
-    core_fibers = lax.all_to_all(core_block, "row", split_axis=0, concat_axis=2, tiled=True)
+    ways, here = (lax.axis_size("row"), lax.axis_index("row"))
+    width = core_block.shape[0] // ways
+    turned = jnp.roll(core_block, -here * width, axis=0)
+    got = [lax.slice_in_dim(turned, 0, width, axis=0)]
+    for far in range(1, ways):
+        sent = lax.slice_in_dim(turned, far * width, (far + 1) * width, axis=0)
+        got.append(lax.ppermute(sent, "row", [(d, (d + far) % ways) for d in range(ways)]))
+    line = jnp.concatenate(got[::-1], axis=2)
+    core_fibers = jnp.roll(line, (here + 1) * got[0].shape[2], axis=2)
     return (core_fibers, basis)
 
 

time: 749 us -> 830 us (1.11); the launches traced: 744 us -> 814 us
  starting transfers between devices: 6.24 us -> 69 us
    ppermute x0 -> x15, starting transfers between devices: none -> 69 us  [shards(): lax.ppermute(sent, 'row', [(d, (d + far) % ways) for d in range(ways)])]
    ppermute x0 -> x15, waiting for transfers between devices: none -> 23.4 us  [shards(): lax.ppermute(sent, 'row', [(d, (d + far) % ways) for d in range(ways)])]
    all_to_all x1 -> x0, waiting for transfers between devices: 16.4 us -> none  [shards(): lax.all_to_all(core_block, 'row', split_axis=0, concat_axis=2, tiled=True)]
  transfers between devices with their start and end apart: 2 -> 16, of which waited for: 2 -> 11; matrix products, arithmetic and copies ran while one was open for 1% -> 1% of each run, Pallas kernels for 0% -> 0%
where the time goes in v1:
time: 830 us; the launch traced here: 814 us
  waiting for transfers between devices  491 us (59%)
  other arithmetic  188 us (23%)
  starting transfers between devices  69 us (8%)
  matrix products  26.8 us (3%)
  between operations  20.2 us (2%)
  local copies, waits for them, and re-layouts  18.4 us (2%)
    psum x1, waiting for transfers between devices, shards(): gram_sum = lax.psum(local_gram, ('row', 'col'))  468 us
    another operation x14, other arithmetic, shards(): basis = power_steps(jnp.linalg.cholesky(gram_sum), start_basis)  78.6 us
    another operation x14, other arithmetic, orthonormalize(): small_lower = jnp.linalg.cholesky(inner_gram)  69.5 us
    ppermute x15, starting transfers between devices, shards(): lax.ppermute(sent, 'row', [(d, (d + far) % ways) for d in range(ways)])  69 us
    another operation x5, other arithmetic, orthonormalize(): jax.scipy.linalg.solve_triangular(small_lower, applied.T, lower=True)  39.4 us
    ppermute x15, waiting for transfers between devices, shards(): lax.ppermute(sent, 'row', [(d, (d + far) % ways) for d in range(ways)])  23.4 us
  transfers between devices with their start and end apart: 16, of which 11 were waited for; matrix products, arithmetic and copies ran while one was open for 1% of the time, Pallas kernels for 0%

profile of v1, /device:TPU:1, one launch (start us, length us, event | category | flops | bytes accessed | tf_op | source)
XLA Modules:
  0.0 813.9 jit_solution(15837007963738050577)
XLA Ops:
  7.2 7.1 fusion.2
  14.4 2.1 copy.27
  16.5 2.3 copy.13
  18.8 468.0 %all-reduce.4.cloned.1.call-done = f32[512,512]{0,1:T(8,128)} async-done(((f32[512,512]{0,1:T(8,128)}), f32[512,512]{0,1:T(8,128)}) %all-reduce.4.cloned.1.call-update) | async-done | bytes 1048592 | tf_op jit(solution)/shard_map/psum | solution.py:39
  486.8 1.6 copy.7
  489.7 11.7 %cholesky.136 = f32[128,128]{1,0:T(8,128)S(1)} custom-call(f32[128,128]{1,0:T(8,128)S(1)} %cholesky.407), custom_call_target="Cholesky" | custom-call | tf_op jit(solution)/shard_map/jit(cholesky)/cholesky | solution.py:40
  501.4 9.8 %custom-call.32 = f32[1,128,128]{1,2,0:T(8,128)S(1)} custom-call(f32[1,128,128]{2,1,0:T(8,128)S(1)} %get-tuple-element.75), custom_call_target="InvertDiagBlocksLowerTriangular" | custom-call | tf_op jit(solution)/shard_map/jit(cholesky)/cholesky | solution.py:40
  513.9 11.7 %cholesky.159 = f32[128,128]{1,0:T(8,128)S(1)} custom-call(f32[128,128]{1,0:T(8,128)S(1)} %cholesky.411), custom_call_target="Cholesky" | custom-call | tf_op jit(solution)/shard_map/jit(cholesky)/cholesky | solution.py:40
  525.6 10.0 %custom-call.33 = f32[1,128,128]{1,2,0:T(8,128)S(1)} custom-call(f32[1,128,128]{2,1,0:T(8,128)S(1)} %get-tuple-element.72), custom_call_target="InvertDiagBlocksLowerTriangular" | custom-call | tf_op jit(solution)/shard_map/jit(cholesky)/cholesky | solution.py:40
  537.2 11.7 %cholesky.294 = f32[128,128]{1,0:T(8,128)S(1)} custom-call(f32[128,128]{1,0:T(8,128)S(1)} %cholesky.416), custom_call_target="Cholesky" | custom-call | tf_op jit(solution)/shard_map/jit(cholesky)/cholesky | solution.py:40
  549.6 9.8 %custom-call.39 = f32[1,128,128]{1,2,0:T(8,128)S(1)} custom-call(f32[1,128,128]{2,1,0:T(8,128)S(1)} %get-tuple-element.69), custom_call_target="InvertDiagBlocksLowerTriangular" | custom-call | tf_op jit(solution)/shard_map/jit(cholesky)/cholesky/custom-call.9 | solution.py:40
  560.8 11.7 %cholesky.307 = f32[128,128]{1,0:T(8,128)S(1)} custom-call(f32[128,128]{1,0:T(8,128)S(1)} %convolution_subtract_fusion.6), custom_call_target="Cholesky" | custom-call | tf_op jit(solution)/shard_map/jit(cholesky)/cholesky | solution.py:40
  576.4 1.6 fusion.16
  580.2 11.7 %cholesky.357 = f32[128,128]{1,0:T(8,128)S(1)} custom-call(f32[128,128]{1,0:T(8,128)S(1)} %cholesky.420), custom_call_target="Cholesky" | custom-call | tf_op jit(solution)/shard_map/jit(cholesky)/cholesky | solution.py:13
  592.6 9.8 %custom-call.40 = f32[1,128,128]{1,2,0:T(8,128)S(1)} custom-call(f32[1,128,128]{2,1,0:T(8,128)S(1)} %get-tuple-element.65), custom_call_target="InvertDiagBlocksLowerTriangular" | custom-call | tf_op jit(solution)/shard_map/jit(cholesky)/cholesky/custom-call.9 | solution.py:13
  603.0 11.9 %cholesky.367 = f32[128,128]{1,0:T(8,128)S(1)} custom-call(f32[128,128]{1,0:T(8,128)S(1)} %convolution_subtract_fusion.5), custom_call_target="Cholesky" | custom-call | tf_op jit(solution)/shard_map/jit(cholesky)/cholesky | solution.py:13
  616.9 3.9 while.4
  620.9 19.7 %custom-call.41 = f32[2,128,128]{1,2,0:T(8,128)S(1)} custom-call(f32[2,128,128]{2,1,0:T(8,128)S(1)} %get-tuple-element.19), custom_call_target="InvertDiagBlocksLowerTriangular" | custom-call | tf_op jit(solution)/shard_map/jit(_solve_triangular)/triangular_solve | solution.py:14
  645.4 11.7 %cholesky.384 = f32[128,128]{1,0:T(8,128)S(1)} custom-call(f32[128,128]{1,0:T(8,128)S(1)} %cholesky.423), custom_call_target="Cholesky" | custom-call | tf_op jit(solution)/shard_map/jit(cholesky)/cholesky | solution.py:13
  657.8 9.8 %custom-call.42 = f32[1,128,128]{1,2,0:T(8,128)S(1)} custom-call(f32[1,128,128]{2,1,0:T(8,128)S(1)} %get-tuple-element.61), custom_call_target="InvertDiagBlocksLowerTriangular" | custom-call | tf_op jit(solution)/shard_map/jit(cholesky)/cholesky/custom-call.9 | solution.py:13
  668.1 11.9 %cholesky.394 = f32[128,128]{1,0:T(8,128)S(1)} custom-call(f32[128,128]{1,0:T(8,128)S(1)} %convolution_subtract_fusion.4), custom_call_target="Cholesky" | custom-call | tf_op jit(solution)/shard_map/jit(cholesky)/cholesky | solution.py:13
  682.1 4.0 while.5
  682.7 1.4 bitcast_dynamic-update-slice_fusion.5
  686.1 19.7 %custom-call.43 = f32[2,128,128]{1,2,0:T(8,128)S(1)} custom-call(f32[2,128,128]{2,1,0:T(8,128)S(1)} %get-tuple-element.20), custom_call_target="InvertDiagBlocksLowerTriangular" | custom-call | tf_op jit(solution)/shard_map/jit(_solve_triangular)/triangular_solve | solution.py:14
  707.2 3.5 fusion.12
  711.1 5.4 collective-permute-start
  717.5 1.9 collective-permute-start.14
  719.4 2.4 collective-permute-start.13
  721.9 3.8 collective-permute-start.12
  725.6 3.0 collective-permute-start.11
  728.6 6.4 collective-permute-start.1
  736.3 2.6 collective-permute-start.2
  739.0 3.6 collective-permute-done.2
  742.5 3.1 collective-permute-start.3
  745.7 1.8 collective-permute-done.3
  747.5 6.1 collective-permute-start.4
  755.0 6.4 collective-permute-start.5
  762.7 6.1 collective-permute-start.6
  768.8 1.9 collective-permute-done.6
  770.7 6.7 collective-permute-start.7
  777.4 1.6 collective-permute-done.7
  779.1 5.5 collective-permute-start.8
  784.6 2.3 collective-permute-done.8
  787.0 5.5 collective-permute-start.9
  792.5 3.7 collective-permute-done.9
  796.2 4.0 collective-permute-start.10
  800.2 4.6 collective-permute-done.10
  805.3 1.6 copy.14
  (119 shorter events, 33.3 us)
Async XLA Ops:
  7.2 569.2 %copy-start = (f32[512,256]{1,0:T(8,128)S(1)}, f32[512,256]{1,0:T(8,128)}, u32[]{:S(2)}) copy-start(f32[512,256]{1,0:T(8,128)} %param.8) | copy-start | bytes 1572868
  7.2 479.6 %all-reduce.4.cloned.1.call-start = ((), (), s32[]{:S(2)}) async-start(), calls=%async_computation | async-start | bytes 2097152 | tf_op jit(solution)/shard_map/psum | solution.py:39
  486.8 1.7 copy-start.1
  488.7 1.0 copy-start.2
  711.1 17.6 %collective-permute-start = (f32[16,8,128]{2,0,1:T(8,128)S(1)}, f32[16,8,128]{2,0,1:T(8,128)S(1)}, u32[]{:S(2)}, u32[]{:S(2)}) collective-permute-start(f32[16,8,128]{2,0,1:T(8,128)S(1)} %get-tuple-element.57), channel_id=1, source_target_pairs={{0,480},{32,0},{64,32},{96,64},{128,96},{160,128},{192,160},{224,1... | collective-permute-start | bytes 196616 | tf_op jit(solution)/shard_map/ppermute | solution.py:51
  717.5 87.4 %collective-permute-start.14 = (f32[16,8,128]{2,0,1:T(8,128)S(1)}, f32[16,8,128]{2,0,1:T(8,128)S(1)}, u32[]{:S(2)}, u32[]{:S(2)}) collective-permute-start(f32[16,8,128]{2,0,1:T(8,128)S(1)} %get-tuple-element.43), channel_id=1, source_target_pairs={{0,32},{32,64},{64,96},{96,128},{128,160},{160,192},{192,224},{224... | collective-permute-start | bytes 196616 | tf_op jit(solution)/shard_map/ppermute | solution.py:51
  719.4 85.4 %collective-permute-start.13 = (f32[16,8,128]{2,0,1:T(8,128)S(1)}, f32[16,8,128]{2,0,1:T(8,128)S(1)}, u32[]{:S(2)}, u32[]{:S(2)}) collective-permute-start(f32[16,8,128]{2,0,1:T(8,128)S(1)} %get-tuple-element.44), channel_id=1, source_target_pairs={{0,64},{32,96},{64,128},{96,160},{128,192},{160,224},{192,256},{22... | collective-permute-start | bytes 196616 | tf_op jit(solution)/shard_map/ppermute | solution.py:51
  721.9 83.0 %collective-permute-start.12 = (f32[16,8,128]{2,0,1:T(8,128)S(1)}, f32[16,8,128]{2,0,1:T(8,128)S(1)}, u32[]{:S(2)}, u32[]{:S(2)}) collective-permute-start(f32[16,8,128]{2,0,1:T(8,128)S(1)} %get-tuple-element.45), channel_id=1, source_target_pairs={{0,96},{32,128},{64,160},{96,192},{128,224},{160,256},{192,288},{2... | collective-permute-start | bytes 196616 | tf_op jit(solution)/shard_map/ppermute | solution.py:51
  725.6 79.2 %collective-permute-start.11 = (f32[16,8,128]{2,0,1:T(8,128)S(1)}, f32[16,8,128]{2,0,1:T(8,128)S(1)}, u32[]{:S(2)}, u32[]{:S(2)}) collective-permute-start(f32[16,8,128]{2,0,1:T(8,128)S(1)} %get-tuple-element.46), channel_id=1, source_target_pairs={{0,128},{32,160},{64,192},{96,224},{128,256},{160,288},{192,320},{... | collective-permute-start | bytes 196616 | tf_op jit(solution)/shard_map/ppermute | solution.py:51
  728.6 7.7 collective-permute-start.1
  736.3 6.2 collective-permute-start.2
  742.5 5.0 collective-permute-start.3
  747.5 7.5 collective-permute-start.4
  755.0 7.7 collective-permute-start.5
  762.7 8.1 collective-permute-start.6
  770.7 8.3 %collective-permute-start.7 = (f32[16,8,128]{2,0,1:T(8,128)S(1)}, f32[16,8,128]{2,0,1:T(8,128)S(1)}, u32[]{:S(2)}, u32[]{:S(2)}) collective-permute-start(f32[16,8,128]{2,0,1:T(8,128)S(1)} %get-tuple-element.50), channel_id=1, source_target_pairs={{0,256},{32,288},{64,320},{96,352},{128,384},{160,416},{192,448},{... | collective-permute-start | bytes 196616 | tf_op jit(solution)/shard_map/ppermute | solution.py:51
  779.1 7.9 collective-permute-start.8
  787.0 9.2 %collective-permute-start.9 = (f32[16,8,128]{2,0,1:T(8,128)S(1)}, f32[16,8,128]{2,0,1:T(8,128)S(1)}, u32[]{:S(2)}, u32[]{:S(2)}) collective-permute-start(f32[16,8,128]{2,0,1:T(8,128)S(1)} %get-tuple-element.48), channel_id=1, source_target_pairs={{0,192},{32,224},{64,256},{96,288},{128,320},{160,352},{192,384},{... | collective-permute-start | bytes 196616 | tf_op jit(solution)/shard_map/ppermute | solution.py:51
  796.2 8.6 %collective-permute-start.10 = (f32[16,8,128]{2,0,1:T(8,128)S(1)}, f32[16,8,128]{2,0,1:T(8,128)S(1)}, u32[]{:S(2)}, u32[]{:S(2)}) collective-permute-start(f32[16,8,128]{2,0,1:T(8,128)S(1)} %get-tuple-element.47), channel_id=1, source_target_pairs={{0,160},{32,192},{64,224},{96,256},{128,288},{160,320},{192,352},{... | collective-permute-start | bytes 196616 | tf_op jit(solution)/shard_map/ppermute | solution.py:51
Sparse Core Ops, SparseCore 0:
  14.5 472.2 all-reduce.3
